TPU v7x, 32 devices: a whole 2x2x4 slice. The times are simulated.
32 devices in a mesh: py: 4 (over z), pz: 8 (over y, x, core).
Axes of the slice: x: 2, y: 2, z: 4, core: 2. Of those that a mesh axis runs over, the one named last changes fastest.
Arguments:
- vort_p: bfloat16 [3, 131072], P(None, ('py', 'pz')), may hold values from -6 to 6
- pair_weights: bfloat16 [8192, 64, 128], P(('py', 'pz')), may hold values from -1.796875 to 1.796875
- pair_part: int32 [8192], P(('py', 'pz')), may hold values from 0 to 31
- pair_node: int32 [8192], P(('py', 'pz')), may hold values from 0 to 95, as said below
- counts: int32 [32], P(('py', 'pz')), may hold values from 128 to 256, as said below
Outputs:
- vel_p: float32 [3, 131072], P(None, ('py', 'pz'))
Inputs may be any that keep to these rules, and one draw needn't show every extreme that they name: `counts`: every pencil has at least 128 live slots, and some pencil has all 256 slots live in every draw. `pair_node`: in every pencil the slots below 96 name each of its node blocks exactly once.
All inputs are finite; a program needn't handle non-finite values.
Results may differ from a plain program's by a relative error of at most 0.0029.
Values sent between devices are 32-bit elements; how exact they have to be, the bound alone decides.
A program may use at most 64 MiB of HBM per device.

v0:
```python
import math
import jax
import jax.numpy as jnp
from jax import lax
from jax.sharding import PartitionSpec as P

NX = 384
CY = 8
CZ = 2
BP = 128
BN = 64
PB_DEV = 32


def twiddle(row_index, col_index, period):
    product = row_index[:, None] * col_index[None, :] % period
    return product.astype(jnp.float32) * (2.0 * math.pi / period)


def forward_table(length):
    angle = twiddle(jnp.arange(length), jnp.arange(length), length)
    cosine = jnp.cos(angle)
    sines = jnp.sin(angle)
    return jnp.stack([jnp.stack([cosine, -sines], 1), jnp.stack([sines, cosine], 1)], 0)


def inverse_table(length):
    angle = twiddle(jnp.arange(length), jnp.arange(length), length)
    cosine = jnp.cos(angle) / length
    sines = jnp.sin(angle) / length
    return jnp.stack([jnp.stack([cosine, sines], 1), jnp.stack([-sines, cosine], 1)], 0)


def cross_terms(coeffs, field):
    return jnp.stack(
        [
            coeffs[1] * field[2] - coeffs[2] * field[1],
            coeffs[2] * field[0] - coeffs[0] * field[2],
            coeffs[0] * field[1] - coeffs[1] * field[0],
        ],
        axis=0,
    )


def signed_wave(length, index):
    signed = jnp.where(index < length // 2, index, index - length)
    return (signed.astype(jnp.float32) * (2.0 * math.pi / length), index == length // 2)


def curl_solve(spectrum, y_cells, z_cells):
    x_local = spectrum.shape[1]
    y_local = spectrum.shape[3]
    mode_x = lax.axis_index("py") * x_local + jnp.arange(x_local)
    wave_x = mode_x.astype(jnp.float32) * (2.0 * math.pi / NX)
    wave_y, edge_y = signed_wave(y_cells, lax.axis_index("pz") * y_local + jnp.arange(y_local))
    wave_z, edge_z = signed_wave(z_cells, jnp.arange(z_cells))
    wave_x3 = wave_x[:, None, None]
    wave_y3 = wave_y[None, :, None]
    wave_z3 = wave_z[None, None, :]
    total = wave_x3 * wave_x3 + wave_y3 * wave_y3 + wave_z3 * wave_z3
    edges = edge_y[None, :, None] | edge_z[None, None, :]
    keep = (total > 0) & jnp.logical_not(edges)
    inverse_sq = jnp.where(keep, 1.0 / jnp.where(keep, total, 1.0), 0.0)
    inv_wave = (wave_x3 * inverse_sq, wave_y3 * inverse_sq, wave_z3 * inverse_sq)
    real_turn = cross_terms(inv_wave, spectrum[:, :, 0])
    imag_turn = cross_terms(inv_wave, spectrum[:, :, 1])
    return jnp.stack([-imag_turn, real_turn], axis=2)


def per_device(vort_p, pair_weights, pair_part, pair_node, counts):
    highest = lax.Precision.HIGHEST
    y_cells = CY * lax.axis_size("py")
    z_cells = CZ * lax.axis_size("pz")
    x_modes = NX // 2
    node_blocks = NX * CY * CZ // BN
    pair_slots = pair_weights.shape[0]
    live_mask = (jnp.arange(pair_slots) < counts[0]).astype(jnp.float32)
    particle_blocks = vort_p.reshape(3, PB_DEV, BP).transpose(1, 0, 2)
    picked = particle_blocks[pair_part]
    products = jnp.einsum("pcq,pnq->pcn", picked, pair_weights, preferred_element_type=jnp.float32)
    products = products * live_mask[:, None, None]
    node_sums = jax.ops.segment_sum(products, pair_node, num_segments=node_blocks)
    vort_grid = node_sums.transpose(1, 0, 2).reshape(3, CZ, CY, NX)
    angle_fwd = twiddle(jnp.arange(NX), jnp.arange(x_modes), NX)
    x_forward = jnp.stack([jnp.cos(angle_fwd), -jnp.sin(angle_fwd)], 1)
    angle_inv = twiddle(jnp.arange(x_modes), jnp.arange(NX), NX)
    mode_weight = (jnp.where(jnp.arange(x_modes) == 0, 1.0, 2.0) / NX)[:, None]
    x_inverse = jnp.stack([mode_weight * jnp.cos(angle_inv), -mode_weight * jnp.sin(angle_inv)], 0)
    y_forward = forward_table(y_cells)
    z_forward = forward_table(z_cells)
    z_inverse = inverse_table(z_cells)
    y_inverse = inverse_table(y_cells)
    x_spectrum = jnp.einsum("czyx,xrm->czrmy", vort_grid, x_forward, precision=highest)
    row_section = jnp.einsum(
        "czrmy,rysk->cmskz",
        lax.all_to_all(x_spectrum, "py", split_axis=3, concat_axis=4, tiled=True),
        y_forward,
        precision=highest,
    )
    col_section = jnp.einsum(
        "cmrkz,rzsw->cmskw",
        lax.all_to_all(row_section, "pz", split_axis=3, concat_axis=4, tiled=True),
        z_forward,
        precision=highest,
    )
    vel_spectrum = curl_solve(col_section, y_cells, z_cells)
    z_back = jnp.einsum("cmrkw,rwsz->cmszk", vel_spectrum, z_inverse, precision=highest)
    y_back = jnp.einsum(
        "cmrzk,rksy->czsym",
        lax.all_to_all(z_back, "pz", split_axis=3, concat_axis=4, tiled=True),
        y_inverse,
        precision=highest,
    )
    vel_grid = jnp.einsum(
        "czrym,rmx->czyx",
        lax.all_to_all(y_back, "py", split_axis=3, concat_axis=4, tiled=True),
        x_inverse,
        precision=highest,
    )
    vel_nodes = vel_grid.astype(jnp.bfloat16).reshape(3, node_blocks, BN).transpose(1, 0, 2)
    chosen = vel_nodes[pair_node]
    back_products = jnp.einsum(
        "pcn,pnq->pcq", chosen, pair_weights, preferred_element_type=jnp.float32
    )
    back_products = back_products * live_mask[:, None, None]
    block_sums = jax.ops.segment_sum(back_products, pair_part, num_segments=PB_DEV)
    return block_sums.transpose(1, 0, 2).reshape(3, PB_DEV * BP)


def solution(mesh):
    placed = (
        P(None, ("py", "pz")),
        P(("py", "pz"), None, None),
        P(("py", "pz")),
        P(("py", "pz")),
        P(("py", "pz")),
    )
    return jax.shard_map(
        per_device, mesh=mesh, in_specs=placed, out_specs=P(None, ("py", "pz")), check_vma=False
    )
```

profile of v0, /device:TPU:0, one launch (start us, length us, event | category | flops | bytes accessed | tf_op | source)
XLA Modules:
  0.0 85.7 jit_solution(18046302165905745508)
XLA Ops:
  0.0 0.0 copy-start
  0.0 1.2 %sine_negate_fusion = (f32[384,1,192]{0,2,1:T(8,128)S(1)}, f32[384,1,192]{0,2,1:T(8,128)S(1)}) fusion(), kind=kLoop, calls=%fused_computation.30 | loop fusion | flops 737280 | bytes 589824 | tf_op jit(solution)/shard_map/neg | solution.py:85
  1.9 0.7 compare_select_fusion.1
  2.6 1.0 %gather_fusion = bf16[256,3,128]{2,1,0:T(4,128)(2,1)S(1)} fusion(bf16[32,3,128]{2,1,0:T(4,128)(2,1)S(1)} %bitcast.162, s32[1024]{0:T(1024)S(1)} %pad_clamp_fusion.1), kind=kCustom, calls=%fused_computation | custom fusion | bytes 394240 | tf_op jit(solution)/shard_map/gather | solution.py:79
  3.6 4.4 %convolution_multiply_fusion.1 = f32[256,3,64]{2,1,0:T(4,128)S(1)} fusion(bf16[256,3,128]{2,1,0:T(4,128)(2,1)S(1)} %gather_fusion, bf16[256,64,128]{2,1,0:T(8,128)(2,1)} %param.6, f32[256]{0:T(256)S(1)} %compare_convert_fusion), kind=kOutput, calls=%fused_computation.5 | convolution fusion | flops 12632064 | bytes 4588544 | tf_op jit(solution)/shard_map/pcq,pnq->pcn/dot_general | solution.py:80
  8.1 0.0 copy-done.2
  8.1 8.3 %scatter_fusion = f32[96,3,64]{2,1,0:T(4,128)S(1)} fusion(f32[96,3,64]{2,1,0:T(4,128)S(1)} %broadcast_in_dim.24, s32[256]{0:T(256)S(1)} %copy-done.2, f32[256,3,64]{2,1,0:T(4,128)S(1)} %convolution_multiply_fusion.1), kind=kCustom, calls=%fused_computation.2 | custom fusion | flops 49152 | bytes 590848 | tf_op jit(solution)/shard_map/scatter-add | solution.py:82
  16.4 0.1 reshape.719
  16.5 0.9 %convolution_bitcast_fusion.4 = f32[3,2,2,192,8]{3,4,1,0,2:T(8,128)S(1)} fusion(f32[3,2,8,384,1]{3,2,1,0,4:T(8,128)S(1)} %reshape.719, f32[384,1,192]{0,2,1:T(8,128)S(1)} %get-tuple-element.19, f32[384,1,192]{0,2,1:T(8,128)S(1)} %get-tuple-element.20), kind=kOutput, calls=%fused_computation.10 | convolution fusion | flops 85082112 | bytes 737280 | tf_op jit(solution)/shard_map/czyx,xrm->czrmy/dot_general | solution.py:93
  17.4 0.8 copy.33
  18.2 2.5 %reshape.735 = f32[4,1,4608]{2,1,0:T(1,128)} reshape(f32[192,2,3,2,8]{4,3,2,1,0:T(2,128)S(1)} %bitcast.163) | data formatting | bytes 147456
  20.7 6.3 %all-to-all-start = ((f32[4,1,4608]{2,1,0:T(1,128)}), f32[4,1,4608]{2,1,0:T(1,128)S(1)}, u32[]{:S(2)}, u32[]{:S(2)}) async-start(f32[4,1,4608]{2,1,0:T(1,128)} %reshape.735), calls=%async_computation | async-start | bytes 147456 | tf_op jit(solution)/shard_map/all_to_all | solution.py:96
  27.0 0.1 fusion.42
  27.1 0.1 fusion.44
  27.2 0.1 fusion.47
  27.2 0.1 fusion.49
  27.4 0.1 broadcast_multiply_fusion.2
  27.4 0.1 fusion.50
  27.5 0.1 broadcast_multiply_fusion
  27.6 0.1 broadcast_add_fusion
  27.7 0.1 or_not_fusion
  27.8 1.2 %sine_multiply_fusion = (f32[1,192,384]{2,1,0:T(8,128)S(1)}, f32[1,192,384]{2,1,0:T(8,128)S(1)}) fusion(f32[192]{0:T(256)S(1)} %fusion.57, f32[192]{0:T(256)S(1)} %fusion.51), kind=kLoop, calls=%fused_computation.25 | loop fusion | flops 811008 | bytes 591360 | tf_op jit(solution)/shard_map/mul | solution.py:88
  29.1 0.1 fusion.46
  29.2 3.6 %all-to-all-done = f32[4,1,4608]{2,1,0:T(1,128)S(1)} async-done(((f32[4,1,4608]{2,1,0:T(1,128)}), f32[4,1,4608]{2,1,0:T(1,128)S(1)}, u32[]{:S(2)}, u32[]{:S(2)}) %all-to-all-start) | async-done | bytes 73760 | tf_op jit(solution)/shard_map/all_to_all | solution.py:96
  32.8 0.5 broadcast.1152
  33.3 0.8 reduce
  34.1 1.8 %reshape.736 = f32[192,2,3,2,8]{4,3,2,1,0:T(2,128)S(1)} reshape(f32[4,4608]{1,0:T(4,128)S(1)} %reduce) | data formatting | bytes 147456
  35.9 0.7 copy.34
  36.6 0.4 convolution_bitcast_fusion.3
  37.0 0.2 copy.81
  37.2 1.0 %reshape.737 = f32[8,1,2304]{2,1,0:T(1,128)} reshape(f32[32,2,3,2,48]{4,3,2,1,0:T(2,128)S(1)} %bitcast.168) | data formatting | bytes 147456
  38.1 3.7 %all-to-all-start.1 = ((f32[8,1,2304]{2,1,0:T(1,128)}), f32[8,1,2304]{2,1,0:T(1,128)S(1)}, u32[]{:S(2)}, u32[]{:S(2)}) async-start(f32[8,1,2304]{2,1,0:T(1,128)} %reshape.737), calls=%async_computation.1 | async-start | bytes 147456 | tf_op jit(solution)/shard_map/all_to_all | solution.py:102
  41.8 5.1 %all-to-all-done.1 = f32[8,1,2304]{2,1,0:T(1,128)S(1)} async-done(((f32[8,1,2304]{2,1,0:T(1,128)}), f32[8,1,2304]{2,1,0:T(1,128)S(1)}, u32[]{:S(2)}, u32[]{:S(2)}) %all-to-all-start.1) | async-done | bytes 73760 | tf_op jit(solution)/shard_map/all_to_all | solution.py:102
  46.9 0.8 reduce.1
  47.7 0.3 reshape.738
  48.1 0.1 copy.36
  48.2 0.4 convolution_bitcast_fusion.2
  48.5 0.1 multiply_subtract_fusion.5
  48.6 0.1 multiply_subtract_fusion.2
  48.8 0.4 convolution_bitcast_fusion.1
  49.2 0.1 copy.80
  49.3 0.9 %reshape.739 = f32[8,1,2304]{2,1,0:T(1,128)} reshape(f32[16,2,3,4,48]{4,3,2,1,0:T(4,128)S(1)} %bitcast.170) | data formatting | bytes 147456
  50.1 3.5 %all-to-all-start.2 = ((f32[8,1,2304]{2,1,0:T(1,128)}), f32[8,1,2304]{2,1,0:T(1,128)S(1)}, u32[]{:S(2)}, u32[]{:S(2)}) async-start(f32[8,1,2304]{2,1,0:T(1,128)} %reshape.739), calls=%async_computation.2 | async-start | bytes 147456 | tf_op jit(solution)/shard_map/all_to_all | solution.py:110
  53.7 4.8 %all-to-all-done.2 = f32[8,1,2304]{2,1,0:T(1,128)S(1)} async-done(((f32[8,1,2304]{2,1,0:T(1,128)}), f32[8,1,2304]{2,1,0:T(1,128)S(1)}, u32[]{:S(2)}, u32[]{:S(2)}) %all-to-all-start.2) | async-done | bytes 73760 | tf_op jit(solution)/shard_map/all_to_all | solution.py:110
  58.5 0.8 reduce.2
  59.3 0.2 reshape.740
  59.5 0.4 convolution_bitcast_fusion
  59.9 0.0 copy-start.3
  59.9 0.2 copy.79
  60.1 1.0 %reshape.741 = f32[4,1,4608]{2,1,0:T(1,128)} reshape(f32[32,2,3,2,48]{4,3,2,1,0:T(2,128)S(1)} %bitcast.172) | data formatting | bytes 147456
  61.0 3.3 %all-to-all-start.3 = ((f32[4,1,4608]{2,1,0:T(1,128)}), f32[4,1,4608]{2,1,0:T(1,128)S(1)}, u32[]{:S(2)}, u32[]{:S(2)}) async-start(f32[4,1,4608]{2,1,0:T(1,128)} %reshape.741), calls=%async_computation.3 | async-start | bytes 147456 | tf_op jit(solution)/shard_map/all_to_all | solution.py:116
  64.4 5.7 %all-to-all-done.3 = f32[4,1,4608]{2,1,0:T(1,128)S(1)} async-done(((f32[4,1,4608]{2,1,0:T(1,128)}), f32[4,1,4608]{2,1,0:T(1,128)S(1)}, u32[]{:S(2)}, u32[]{:S(2)}) %all-to-all-start.3) | async-done | bytes 73760 | tf_op jit(solution)/shard_map/all_to_all | solution.py:116
  70.1 0.8 reduce.3
  70.9 0.3 reshape.742
  71.3 0.1 copy.77
  71.4 0.1 all_to_all.67
  71.5 0.5 fusion
  72.0 0.1 reshape.680
  72.1 0.1 copy.78
  72.2 1.0 %gather_fusion.1 = bf16[256,3,64]{2,1,0:T(4,128)(2,1)S(1)} fusion(bf16[96,3,64]{2,1,0:T(4,128)(2,1)S(1)} %bitcast.166, s32[1024]{0:T(1024)S(1)} %pad_clamp_fusion), kind=kCustom, calls=%fused_computation.1 | custom fusion | bytes 197632 | tf_op jit(solution)/shard_map/gather | solution.py:121
  73.2 3.4 %convolution_multiply_fusion = f32[256,3,128]{2,1,0:T(4,128)S(1)} fusion(bf16[256,3,64]{2,1,0:T(4,128)(2,1)S(1)} %gather_fusion.1, bf16[256,64,128]{2,1,0:T(8,128)(2,1)} %param.6, f32[256]{0:T(256)S(1)} %compare_convert_fusion), kind=kOutput, calls=%fused_computation.4 | convolution fusion | flops 12681216 | bytes 4686848 | tf_op jit(solution)/shard_map/pcn,pnq->pcq/dot_general | solution.py:122
  76.6 8.4 %scatter_fusion.1 = f32[32,3,128]{2,1,0:T(4,128)S(1)} fusion(f32[32,3,128]{2,1,0:T(4,128)S(1)} %broadcast_in_dim.22, s32[256]{0:T(256)S(1)} %copy-done.3, f32[256,3,128]{2,1,0:T(4,128)S(1)} %convolution_multiply_fusion), kind=kCustom, calls=%fused_computation.3 | custom fusion | flops 98304 | bytes 1180672 | tf_op jit(solution)/shard_map/scatter-add | solution.py:126
  85.1 0.0 copy-start.1
  85.1 0.6 copy-done.1
  (24 shorter events, 0.2 us)
Async XLA Ops:
  0.0 2.6 %copy-start = (bf16[3,4096]{1,0:T(4,128)(2,1)S(1)}, bf16[3,4096]{1,0:T(4,128)(2,1)}, u32[]{:S(2)}) copy-start(bf16[3,4096]{1,0:T(4,128)(2,1)} %param.5) | copy-start | bytes 73732
  0.0 8.1 %copy-start.2 = (s32[256]{0:T(256)S(1)}, s32[256]{0:T(256)}, u32[]{:S(2)}) copy-start(s32[256]{0:T(256)} %param.8) | copy-start | bytes 3076
  20.7 12.1 %all-to-all-start = ((f32[4,1,4608]{2,1,0:T(1,128)}), f32[4,1,4608]{2,1,0:T(1,128)S(1)}, u32[]{:S(2)}, u32[]{:S(2)}) async-start(f32[4,1,4608]{2,1,0:T(1,128)} %reshape.735), calls=%async_computation | async-start | bytes 147456 | tf_op jit(solution)/shard_map/all_to_all | solution.py:96
  38.1 8.8 %all-to-all-start.1 = ((f32[8,1,2304]{2,1,0:T(1,128)}), f32[8,1,2304]{2,1,0:T(1,128)S(1)}, u32[]{:S(2)}, u32[]{:S(2)}) async-start(f32[8,1,2304]{2,1,0:T(1,128)} %reshape.737), calls=%async_computation.1 | async-start | bytes 147456 | tf_op jit(solution)/shard_map/all_to_all | solution.py:102
  50.1 8.4 %all-to-all-start.2 = ((f32[8,1,2304]{2,1,0:T(1,128)}), f32[8,1,2304]{2,1,0:T(1,128)S(1)}, u32[]{:S(2)}, u32[]{:S(2)}) async-start(f32[8,1,2304]{2,1,0:T(1,128)} %reshape.739), calls=%async_computation.2 | async-start | bytes 147456 | tf_op jit(solution)/shard_map/all_to_all | solution.py:110
  59.9 16.7 %copy-start.3 = (s32[256]{0:T(256)S(1)}, s32[256]{0:T(256)}, u32[]{:S(2)}) copy-start(s32[256]{0:T(256)} %param.7) | copy-start | bytes 3076
  61.0 9.0 %all-to-all-start.3 = ((f32[4,1,4608]{2,1,0:T(1,128)}), f32[4,1,4608]{2,1,0:T(1,128)S(1)}, u32[]{:S(2)}, u32[]{:S(2)}) async-start(f32[4,1,4608]{2,1,0:T(1,128)} %reshape.741), calls=%async_computation.3 | async-start | bytes 147456 | tf_op jit(solution)/shard_map/all_to_all | solution.py:116
  85.1 0.6 copy-start.1
where the time goes:
time: 86.3 us; the launch traced here: 85.7 us
  other arithmetic  24.3 us (28%)
  waiting for transfers between devices  19.2 us (22%)
  starting transfers between devices  16.9 us (20%)
  local copies, waits for them, and re-layouts  13.6 us (16%)
  matrix products  10.6 us (12%)
  between operations  1.09 us (1%)
    unnamed x16, local copies, waits for them, and re-layouts  8.58 us
    scatter-add x1, other arithmetic, per_device(): jax.ops.segment_sum(back_products, pair_part, num_segments=PB_DEV)  8.45 us
    scatter-add x1, other arithmetic, per_device(): jax.ops.segment_sum(products, pair_node, num_segments=node_blocks)  8.34 us
    all_to_all x1, starting transfers between devices, per_device(): lax.all_to_all(x_spectrum, 'py', split_axis=3, concat_axis=4, tiled=True)  6.33 us
    all_to_all x1, waiting for transfers between devices, per_device(): lax.all_to_all(y_back, 'py', split_axis=3, concat_axis=4, tiled=True)  5.72 us
    all_to_all x1, waiting for transfers between devices, per_device(): lax.all_to_all(row_section, 'pz', split_axis=3, concat_axis=4, tiled=True)  5.05 us
    all_to_all x1, waiting for transfers between devices, per_device(): lax.all_to_all(z_back, 'pz', split_axis=3, concat_axis=4, tiled=True)  4.8 us
    dot_general x1, matrix products, per_device(): jnp.einsum('pcq,pnq->pcn', picked, pair_weights, preferred_element_type=j...  4.45 us
  transfers between devices with their start and end apart: 4, of which 4 were waited for; matrix products, arithmetic and copies ran while one was open for 2% of the time, Pallas kernels for 0%

commit v1 on v0

--- a/solution.py
+++ b/solution.py
@@ -99,7 +99,12 @@
     )
     col_section = jnp.einsum(
         "cmrkz,rzsw->cmskw",
-        lax.all_to_all(row_section, "pz", split_axis=3, concat_axis=4, tiled=True),
+        jnp.concatenate(
+            lax.all_to_all(
+                jnp.stack(jnp.split(row_section, lax.axis_size("pz"), axis=3)), "pz", 0, 0
+            ),
+            axis=4,
+        ),
         z_forward,
         precision=highest,
     )

time: 86.3 us -> 86.9 us (level)
    all_to_all x1, waiting for transfers between devices: 5.72 us -> 4.31 us  [per_device(): lax.all_to_all(y_back, 'py', split_axis=3, concat_axis=4, tiled=True)]
    all_to_all x1, waiting for transfers between devices: 3.62 us -> 4.87 us  [per_device(): lax.all_to_all(x_spectrum, 'py', split_axis=3, concat_axis=4, tiled=True)]
    unnamed x16 -> x23, local copies, waits for them, and re-layouts: 8.58 us -> 8.44 us
where the time goes in v1:
time: 86.9 us; the launch traced here: 86.3 us
  other arithmetic  24.9 us (29%)
  waiting for transfers between devices  19.2 us (22%)
  starting transfers between devices  17 us (20%)
  local copies, waits for them, and re-layouts  13.4 us (15%)
  matrix products  10.6 us (12%)
  between operations  1.13 us (1%)
    scatter-add x1, other arithmetic, per_device(): jax.ops.segment_sum(back_products, pair_part, num_segments=PB_DEV)  8.45 us
    unnamed x23, local copies, waits for them, and re-layouts  8.44 us
    scatter-add x1, other arithmetic, per_device(): jax.ops.segment_sum(products, pair_node, num_segments=node_blocks)  8.34 us
    all_to_all x1, starting transfers between devices, per_device(): lax.all_to_all(x_spectrum, 'py', split_axis=3, concat_axis=4, tiled=True)  6.33 us
    all_to_all x1, waiting for transfers between devices, per_device(): lax.all_to_all(jnp.stack(jnp.split(row_section, lax.axis_size('pz'), axis...  5.06 us
    all_to_all x1, waiting for transfers between devices, per_device(): lax.all_to_all(z_back, 'pz', split_axis=3, concat_axis=4, tiled=True)  4.98 us
    all_to_all x1, waiting for transfers between devices, per_device(): lax.all_to_all(x_spectrum, 'py', split_axis=3, concat_axis=4, tiled=True)  4.87 us
    dot_general x1, matrix products, per_device(): jnp.einsum('pcq,pnq->pcn', picked, pair_weights, preferred_element_type=j...  4.45 us
  transfers between devices with their start and end apart: 4, of which 4 were waited for; matrix products, arithmetic and copies ran while one was open for 2% of the time, Pallas kernels for 0%

profile of v1, /device:TPU:0, one launch (start us, length us, event | category | flops | bytes accessed | tf_op | source)
XLA Modules:
  0.0 86.3 jit_solution(4747821130605971579)
XLA Ops:
  0.0 0.0 copy-start
  0.0 1.2 %sine_negate_fusion = (f32[384,1,192]{0,2,1:T(8,128)S(1)}, f32[384,1,192]{0,2,1:T(8,128)S(1)}) fusion(), kind=kLoop, calls=%fused_computation.30 | loop fusion | flops 737280 | bytes 589824 | tf_op jit(solution)/shard_map/neg | solution.py:85
  1.2 0.7 compare_select_fusion
  1.9 0.7 compare_select_fusion.1
  3.3 0.0 copy-done
  3.3 1.0 %gather_fusion = bf16[256,3,128]{2,1,0:T(4,128)(2,1)S(1)} fusion(bf16[32,3,128]{2,1,0:T(4,128)(2,1)S(1)} %bitcast.192, s32[1024]{0:T(1024)S(1)} %get-tuple-element.20), kind=kCustom, calls=%fused_computation | custom fusion | bytes 394240 | tf_op jit(solution)/shard_map/gather | solution.py:79
  4.3 4.4 %convolution_multiply_fusion.1 = f32[256,3,64]{2,1,0:T(4,128)S(1)} fusion(bf16[256,3,128]{2,1,0:T(4,128)(2,1)S(1)} %gather_fusion, bf16[256,64,128]{2,1,0:T(8,128)(2,1)} %param.6, f32[256]{0:T(256)S(1)} %compare_convert_fusion), kind=kOutput, calls=%fused_computation.5 | convolution fusion | flops 12632064 | bytes 4588544 | tf_op jit(solution)/shard_map/pcq,pnq->pcn/dot_general | solution.py:80
  8.8 8.3 %scatter_fusion = f32[96,3,64]{2,1,0:T(4,128)S(1)} fusion(f32[96,3,64]{2,1,0:T(4,128)S(1)} %broadcast_in_dim.24, s32[256]{0:T(256)S(1)} %copy-done.2, f32[256,3,64]{2,1,0:T(4,128)S(1)} %convolution_multiply_fusion.1), kind=kCustom, calls=%fused_computation.2 | custom fusion | flops 49152 | bytes 590848 | tf_op jit(solution)/shard_map/scatter-add | solution.py:82
  17.1 0.1 reshape.727
  17.2 0.9 convolution_bitcast_fusion.4
  18.1 0.8 copy.33
  18.9 2.5 %reshape.743 = f32[4,1,4608]{2,1,0:T(1,128)} reshape(f32[192,2,3,2,8]{4,3,2,1,0:T(2,128)S(1)} %bitcast.193) | data formatting | bytes 147456
  21.4 6.3 %all-to-all-start = ((f32[4,1,4608]{2,1,0:T(1,128)}), f32[4,1,4608]{2,1,0:T(1,128)S(1)}, u32[]{:S(2)}, u32[]{:S(2)}) async-start(f32[4,1,4608]{2,1,0:T(1,128)} %reshape.743), calls=%async_computation | async-start | bytes 147456 | tf_op jit(solution)/shard_map/all_to_all | solution.py:96
  27.7 0.1 fusion.52
  27.8 0.1 fusion.54
  27.9 0.1 fusion.57
  27.9 0.1 fusion.59
  28.1 0.1 broadcast_multiply_fusion.2
  28.1 0.1 fusion.60
  28.2 0.1 broadcast_multiply_fusion
  28.3 0.1 fusion.56
  28.4 0.1 broadcast_add_fusion
  28.5 0.1 or_not_fusion
  28.6 4.9 %all-to-all-done = f32[4,1,4608]{2,1,0:T(1,128)S(1)} async-done(((f32[4,1,4608]{2,1,0:T(1,128)}), f32[4,1,4608]{2,1,0:T(1,128)S(1)}, u32[]{:S(2)}, u32[]{:S(2)}) %all-to-all-start) | async-done | bytes 73760 | tf_op jit(solution)/shard_map/all_to_all | solution.py:96
  33.5 0.5 broadcast.1152
  34.0 0.8 reduce
  34.8 1.8 %reshape.744 = f32[192,2,3,2,8]{4,3,2,1,0:T(2,128)S(1)} reshape(f32[4,4608]{1,0:T(4,128)S(1)} %reduce) | data formatting | bytes 147456
  36.6 0.7 copy.34
  37.3 0.4 convolution_bitcast_fusion.3
  37.9 0.9 reshape.745
  38.7 3.7 %all-to-all-start.1 = ((f32[8,1,2304]{2,1,0:T(1,128)}), f32[8,1,2304]{2,1,0:T(1,128)S(1)}, u32[]{:S(2)}, u32[]{:S(2)}) async-start(f32[8,1,2304]{2,1,0:T(1,128)} %reshape.745), calls=%async_computation.1 | async-start | bytes 147456 | tf_op jit(solution)/shard_map/all_to_all | solution.py:103
  42.4 5.1 %all-to-all-done.1 = f32[8,1,2304]{2,1,0:T(1,128)S(1)} async-done(((f32[8,1,2304]{2,1,0:T(1,128)}), f32[8,1,2304]{2,1,0:T(1,128)S(1)}, u32[]{:S(2)}, u32[]{:S(2)}) %all-to-all-start.1) | async-done | bytes 73760 | tf_op jit(solution)/shard_map/all_to_all | solution.py:103
  47.5 0.8 reduce.1
  48.3 0.2 reshape.746
  48.6 0.1 copy.35
  48.7 0.4 convolution_bitcast_fusion.2
  49.0 0.1 multiply_subtract_fusion.5
  49.1 0.1 multiply_subtract_fusion.2
  49.3 0.4 convolution_bitcast_fusion.1
  49.7 0.1 copy.83
  49.8 0.9 reshape.747
  50.6 3.4 %all-to-all-start.2 = ((f32[8,1,2304]{2,1,0:T(1,128)}), f32[8,1,2304]{2,1,0:T(1,128)S(1)}, u32[]{:S(2)}, u32[]{:S(2)}) async-start(f32[8,1,2304]{2,1,0:T(1,128)} %reshape.747), calls=%async_computation.2 | async-start | bytes 147456 | tf_op jit(solution)/shard_map/all_to_all | solution.py:115
  54.0 5.0 %all-to-all-done.2 = f32[8,1,2304]{2,1,0:T(1,128)S(1)} async-done(((f32[8,1,2304]{2,1,0:T(1,128)}), f32[8,1,2304]{2,1,0:T(1,128)S(1)}, u32[]{:S(2)}, u32[]{:S(2)}) %all-to-all-start.2) | async-done | bytes 73760 | tf_op jit(solution)/shard_map/all_to_all | solution.py:115
  59.0 0.8 reduce.2
  59.8 0.2 reshape.748
  60.0 0.4 convolution_bitcast_fusion
  60.4 0.2 copy.82
  60.6 0.9 %reshape.749 = f32[4,1,4608]{2,1,0:T(1,128)} reshape(f32[32,2,3,2,48]{4,3,2,1,0:T(2,128)S(1)} %bitcast.200) | data formatting | bytes 147456
  61.5 3.6 %all-to-all-start.3 = ((f32[4,1,4608]{2,1,0:T(1,128)}), f32[4,1,4608]{2,1,0:T(1,128)S(1)}, u32[]{:S(2)}, u32[]{:S(2)}) async-start(f32[4,1,4608]{2,1,0:T(1,128)} %reshape.749), calls=%async_computation.3 | async-start | bytes 147456 | tf_op jit(solution)/shard_map/all_to_all | solution.py:121
  65.2 1.2 %sine_multiply_fusion = (f32[1,192,384]{2,1,0:T(8,128)S(1)}, f32[1,192,384]{2,1,0:T(8,128)S(1)}) fusion(f32[192]{0:T(256)S(1)} %fusion.67, f32[192]{0:T(256)S(1)} %fusion.61), kind=kLoop, calls=%fused_computation.25 | loop fusion | flops 811008 | bytes 591360 | tf_op jit(solution)/shard_map/mul | solution.py:88
  66.4 4.3 %all-to-all-done.3 = f32[4,1,4608]{2,1,0:T(1,128)S(1)} async-done(((f32[4,1,4608]{2,1,0:T(1,128)}), f32[4,1,4608]{2,1,0:T(1,128)S(1)}, u32[]{:S(2)}, u32[]{:S(2)}) %all-to-all-start.3) | async-done | bytes 73760 | tf_op jit(solution)/shard_map/all_to_all | solution.py:121
  70.7 0.8 reduce.3
  71.5 0.3 reshape.750
  71.9 0.1 copy.80
  72.0 0.1 all_to_all.54
  72.2 0.5 fusion
  72.6 0.1 reshape.688
  72.8 0.1 copy.81
  72.8 1.0 %gather_fusion.1 = bf16[256,3,64]{2,1,0:T(4,128)(2,1)S(1)} fusion(bf16[96,3,64]{2,1,0:T(4,128)(2,1)S(1)} %bitcast.196, s32[1024]{0:T(1024)S(1)} %get-tuple-element.19), kind=kCustom, calls=%fused_computation.1 | custom fusion | bytes 197632 | tf_op jit(solution)/shard_map/gather | solution.py:126
  73.8 3.4 %convolution_multiply_fusion = f32[256,3,128]{2,1,0:T(4,128)S(1)} fusion(bf16[256,3,64]{2,1,0:T(4,128)(2,1)S(1)} %gather_fusion.1, bf16[256,64,128]{2,1,0:T(8,128)(2,1)} %param.6, f32[256]{0:T(256)S(1)} %compare_convert_fusion), kind=kOutput, calls=%fused_computation.4 | convolution fusion | flops 12681216 | bytes 4686848 | tf_op jit(solution)/shard_map/pcn,pnq->pcq/dot_general | solution.py:127
  77.2 0.0 copy-done.3
  77.2 8.4 %scatter_fusion.1 = f32[32,3,128]{2,1,0:T(4,128)S(1)} fusion(f32[32,3,128]{2,1,0:T(4,128)S(1)} %broadcast_in_dim.22, s32[256]{0:T(256)S(1)} %copy-done.3, f32[256,3,128]{2,1,0:T(4,128)S(1)} %convolution_multiply_fusion), kind=kCustom, calls=%fused_computation.3 | custom fusion | flops 98304 | bytes 1180672 | tf_op jit(solution)/shard_map/scatter-add | solution.py:131
  85.7 0.0 copy-start.1
  85.7 0.6 copy-done.1
  (31 shorter events, 0.4 us)
Async XLA Ops:
  0.0 3.3 %copy-start = (bf16[3,4096]{1,0:T(4,128)(2,1)S(1)}, bf16[3,4096]{1,0:T(4,128)(2,1)}, u32[]{:S(2)}) copy-start(bf16[3,4096]{1,0:T(4,128)(2,1)} %param.5) | copy-start | bytes 73732
  0.0 8.8 %copy-start.2 = (s32[256]{0:T(256)S(1)}, s32[256]{0:T(256)}, u32[]{:S(2)}) copy-start(s32[256]{0:T(256)} %param.8) | copy-start | bytes 3076
  21.4 12.1 %all-to-all-start = ((f32[4,1,4608]{2,1,0:T(1,128)}), f32[4,1,4608]{2,1,0:T(1,128)S(1)}, u32[]{:S(2)}, u32[]{:S(2)}) async-start(f32[4,1,4608]{2,1,0:T(1,128)} %reshape.743), calls=%async_computation | async-start | bytes 147456 | tf_op jit(solution)/shard_map/all_to_all | solution.py:96
  38.7 8.8 %all-to-all-start.1 = ((f32[8,1,2304]{2,1,0:T(1,128)}), f32[8,1,2304]{2,1,0:T(1,128)S(1)}, u32[]{:S(2)}, u32[]{:S(2)}) async-start(f32[8,1,2304]{2,1,0:T(1,128)} %reshape.745), calls=%async_computation.1 | async-start | bytes 147456 | tf_op jit(solution)/shard_map/all_to_all | solution.py:103
  50.6 8.4 %all-to-all-start.2 = ((f32[8,1,2304]{2,1,0:T(1,128)}), f32[8,1,2304]{2,1,0:T(1,128)S(1)}, u32[]{:S(2)}, u32[]{:S(2)}) async-start(f32[8,1,2304]{2,1,0:T(1,128)} %reshape.747), calls=%async_computation.2 | async-start | bytes 147456 | tf_op jit(solution)/shard_map/all_to_all | solution.py:115
  61.5 15.7 %copy-start.3 = (s32[256]{0:T(256)S(1)}, s32[256]{0:T(256)}, u32[]{:S(2)}) copy-start(s32[256]{0:T(256)} %param.7) | copy-start | bytes 3076
  61.5 9.2 %all-to-all-start.3 = ((f32[4,1,4608]{2,1,0:T(1,128)}), f32[4,1,4608]{2,1,0:T(1,128)S(1)}, u32[]{:S(2)}, u32[]{:S(2)}) async-start(f32[4,1,4608]{2,1,0:T(1,128)} %reshape.749), calls=%async_computation.3 | async-start | bytes 147456 | tf_op jit(solution)/shard_map/all_to_all | solution.py:121
  85.7 0.6 copy-start.1
